TPU v7x, 32 devices: a whole 2x2x4 slice. The times are simulated.
32 devices in a mesh: parts: 2 (over y), seg: 4 (over z), grp: 4 (over x, core).
Axes of the slice: x: 2, y: 2, z: 4, core: 2. Of those that a mesh axis runs over, the one named last changes fastest.
Arguments:
- env_left: bfloat16 [8, 4, 30, 192, 192], P(('parts', 'seg'), 'grp'), parts along dimension 0, may hold values from -1 to 2
- env_right: bfloat16 [8, 4, 30, 192, 192], P(('parts', 'seg'), 'grp'), parts along dimension 0, may hold values from -1 to 2
- site_left: bfloat16 [8, 4, 192, 192], P(('parts', 'seg'), 'grp'), parts along dimension 0, may hold values from -6 to 6
- site_right: bfloat16 [8, 4, 192, 192], P(('parts', 'seg'), 'grp'), parts along dimension 0, may hold values from -2 to 2
- bond_weights: float32 [8, 4, 192], P(('parts', 'seg'), 'grp'), parts along dimension 0, may hold values from 0.5 to 2
- mpo_charge: int32 [8, 30], P(('parts', 'seg')), parts along dimension 0, may hold values from -1 to 1, as said below
- sector_rows: int32 [8, 4], P(('parts', 'seg'), 'grp'), parts along dimension 0, may hold values from 1 to 192, 576 in all within a row
Outputs:
- theta_new: float32 [8, 4, 192, 192], P(('parts', 'seg'), 'grp'), parts along dimension 0
- energy: float32 [8], P(('parts', 'seg')), parts along dimension 0
There are 2 independent parts, one for each index of `parts`. A program takes and returns all parts, laid end to end along the dimension named above; each array names one. Nothing has to cross between parts.
Inputs may be any that keep to these rules, and one draw needn't show every extreme that they name: `sector_rows`: for each segment the 4 values sum to 576 and the largest is 192. `mpo_charge`: for each segment exactly 10 of the 30 values are -1, exactly 10 are +1, the rest 0.
All inputs are finite; a program needn't handle non-finite values. No bound on the sum of `sector_rows` on one device may be relied on, other than what follows from the above.
Results may differ from a plain program's by a relative error of at most 0.0054.
Values may be sent and summed in bfloat16 or wider, within the bound.
A program may use at most 64 MiB of HBM per device.

v0:
```python
import jax
import jax.numpy as jnp
from jax import lax
from jax.sharding import PartitionSpec as P

eps_value = 1e-06


def from_behind(block, axis, distance):
    devices = range(lax.axis_size(axis))
    route = [(i - distance, i) for i in devices if i - distance in devices]
    return lax.ppermute(block, axis, route)


def body(env_left, env_right, site_left, site_right, bond_weights, mpo_charge, sector_rows):
    mpo_width = env_left.shape[2]
    block_size = env_left.shape[3]
    sectors = lax.axis_size("grp")
    entry_count = float(sectors * block_size * block_size)
    charged = mpo_width // 3
    scaled = (site_left.astype(jnp.float32) / bond_weights[:, :, None, :]).astype(jnp.bfloat16)
    got_env, got_edge = from_behind((env_left, scaled), "seg", 1)
    first_seg = lax.axis_index("seg") == 0
    eye_block = jnp.eye(block_size, dtype=jnp.bfloat16)
    vacuum = jnp.where(
        lax.broadcasted_iota(jnp.int32, (mpo_width, 1, 1), 0) == 0,
        eye_block[None],
        jnp.zeros((1, block_size, block_size), jnp.bfloat16),
    )
    left_env = jnp.where(first_seg, vacuum, got_env[0, 0])
    edge_tensor = jnp.where(first_seg, eye_block, got_edge[0, 0])
    live_rows = (lax.broadcasted_iota(jnp.int32, (block_size, 1), 0) < sector_rows[0, 0]).astype(
        jnp.float32
    )
    theta_vec = (
        jnp.dot(edge_tensor, site_right[0, 0], preferred_element_type=jnp.float32) * live_rows
    )
    charges = mpo_charge[0]
    ordering = jnp.argsort(charges, stable=True)
    left_sorted = jnp.take(left_env, ordering, axis=0)
    right_sorted = jnp.take(env_right[0, 0], ordering, axis=0)
    bounds = ((0, charged), (charged, mpo_width - charged), (mpo_width - charged, mpo_width))

    def grp_means(values):
        return lax.psum(jnp.stack(values), "grp") / entry_count

    def matvec(vector):
        rounded = vector.astype(jnp.bfloat16)
        inner_prod = jnp.einsum(
            "wab,bc->wac", left_sorted, rounded, preferred_element_type=jnp.float32
        ).astype(jnp.bfloat16)
        slabs = [
            jnp.einsum(
                "wac,wcd->ad",
                inner_prod[lo:hi],
                right_sorted[lo:hi],
                preferred_element_type=jnp.float32,
            ).astype(jnp.bfloat16)
            for lo, hi in bounds
        ]
        from_below = from_behind(slabs[2], "grp", 1)
        from_above = from_behind(slabs[0], "grp", -1)
        own_sector = (
            slabs[1].astype(jnp.float32)
            + from_below.astype(jnp.float32)
            + from_above.astype(jnp.float32)
        )
        return own_sector * live_rows

    basis_one = theta_vec / jnp.sqrt(grp_means([jnp.sum(theta_vec * theta_vec)])[0] + eps_value)
    image_one = matvec(basis_one)
    diag_one = grp_means([jnp.sum(basis_one * image_one)])[0]
    residual = image_one - diag_one * basis_one
    res_norm = grp_means([jnp.sum(residual * residual)])[0]
    basis_two = residual / jnp.sqrt(res_norm + eps_value)
    image_two = matvec(basis_two)
    ritz_terms = grp_means([jnp.sum(basis_two * image_one), jnp.sum(basis_two * image_two)])
    coupling = ritz_terms[0]
    diag_two = ritz_terms[1]
    half_gap = 0.5 * (diag_one - diag_two)
    energy = 0.5 * (diag_one + diag_two) - jnp.sqrt(half_gap * half_gap + coupling * coupling)
    lead_coef = diag_two - energy
    norm_scale = jnp.sqrt(lead_coef * lead_coef + coupling * coupling)
    theta_new = (lead_coef * basis_one - coupling * basis_two) / norm_scale
    return (theta_new[None, None], energy[None])


def solution(mesh):
    return jax.shard_map(
        body,
        mesh=mesh,
        in_specs=(
            P(("parts", "seg"), "grp", None, None, None),
            P(("parts", "seg"), "grp", None, None, None),
            P(("parts", "seg"), "grp", None, None),
            P(("parts", "seg"), "grp", None, None),
            P(("parts", "seg"), "grp", None),
            P(("parts", "seg"), None),
            P(("parts", "seg"), "grp"),
        ),
        out_specs=(P(("parts", "seg"), "grp", None, None), P(("parts", "seg"))),
        check_vma=False,
    )
```

profile of v0, /device:TPU:0, one launch (start us, length us, event | category | flops | bytes accessed | tf_op | source)
XLA Modules:
  0.0 144.2 jit_solution(13690356448737179420)
XLA Ops:
  0.6 6.8 %collective-permute-start = (bf16[1,1,30,192,192]{4,3,2,1,0:T(8,128)(2,1)}, bf16[1,1,30,192,192]{4,3,2,1,0:T(8,128)(2,1)}, u32[]{:S(2)}, u32[]{:S(2)}) collective-permute-start(bf16[1,1,30,192,192]{4,3,2,1,0:T(8,128)(2,1)} %param.9), channel_id=1, source_target_pairs={{0,4},{4,8},{8,12},{1,5},{5,9},{9,13},{2,6},{6,10},{10,14},{3,7},{... | collective-permute-start | bytes 6635528 | tf_op jit(solution)/shard_map/ppermute | solution.py:12
  7.4 0.9 divide_convert_fusion
  8.4 1.9 %collective-permute-start.1 = (bf16[1,1,192,192]{3,2,1,0:T(8,128)(2,1)S(1)}, bf16[1,1,192,192]{3,2,1,0:T(8,128)(2,1)S(1)}, u32[]{:S(2)}, u32[]{:S(2)}) collective-permute-start(bf16[1,1,192,192]{3,2,1,0:T(8,128)(2,1)S(1)} %divide_convert_fusion), channel_id=1, source_target_pairs={{0,4},{4,8},{8,12},{1,5},{5,9},{9,13},{2,6},{6,10},{10,14},{3,7},{... | collective-permute-start | bytes 221192 | tf_op jit(solution)/shard_map/ppermute | solution.py:12
  10.9 2.3 %sort.17 = (s32[30]{0:T(128)}, s32[30]{0:T(128)S(1)}) sort(s32[30]{0:T(128)} %bitcast.72, s32[30]{0:T(128)S(1)} %iota.39), dimensions={0}, to_apply=%region_0.1 | sort | flops 150 | bytes 480 | tf_op jit(solution)/shard_map/jit(argsort)/sort | solution.py:39
  13.2 2.4 %gather_fusion.1 = bf16[30,192,192]{2,1,0:T(8,128)(2,1)} fusion(bf16[30,192,192]{2,1,0:T(8,128)(2,1)S(1)} %bitcast.70, s32[1024]{0:T(1024)S(1)} %pad_clamp_fusion), kind=kCustom, calls=%fused_computation.1.clone | custom fusion | bytes 4423800 | tf_op jit(solution)/shard_map/jit(_take)/gather | solution.py:41
  15.7 3.9 %broadcast_select_fusion = bf16[30,192,192]{2,1,0:T(8,128)(2,1)} fusion(bf16[30,192,192]{2,1,0:T(8,128)(2,1)} %gather_fusion.1, pred[30]{0:T(512)(128)(4,1)S(1)} %compare_and_fusion), kind=kLoop, calls=%fused_computation.3 | loop fusion | flops 1105920 | bytes 4423710 | tf_op jit(solution)/shard_map/jit(_take)/select_n | solution.py:41
  19.5 51.8 %collective-permute-done.1 = bf16[1,1,192,192]{3,2,1,0:T(8,128)(2,1)S(1)} collective-permute-done((bf16[1,1,192,192]{3,2,1,0:T(8,128)(2,1)S(1)}, bf16[1,1,192,192]{3,2,1,0:T(8,128)(2,1)S(1)}, u32[]{:S(2)}, u32[]{:S(2)}) %collective-permute-start.1) | collective-permute-done | bytes 73760 | tf_op jit(solution)/shard_map/ppermute | solution.py:12
  71.3 0.8 multiply_reduce_fusion.4
  72.1 6.3 %psum.28 = f32[1]{0:T(128)} all-reduce(f32[1]{0:T(128)} %bitcast.6), channel_id=1, replica_groups=mesh['parts'=2,'seg'=4,'grp'=4] {'grp'}, use_global_device_ids=true, to_apply=%region_2.4 | all-reduce | flops 1 | bytes 8 | tf_op jit(solution)/shard_map/psum | solution.py:45
  79.1 3.8 %bitcast_select_fusion = bf16[30,192,192]{2,1,0:T(8,128)(2,1)} fusion(bf16[1,1,30,192,192]{4,3,2,1,0:T(8,128)(2,1)} %collective-permute-done, pred[30]{0:T(512)(128)(4,1)S(1)} %iota_compare_fusion.2, pred[]{:T(512)S(6)} %eq.27, bf16[192,192]{1,0:T(8,128)(2,1)S(1)} %fusion.14), kind=kLoop, calls=%fused_computation.2 | loop fusion | flops 2211840 | bytes 4497439 | tf_op jit(solution)/shard_map/jit(_where)/select_n | solution.py:30
  82.9 4.2 %gather_fusion = bf16[30,192,192]{2,1,0:T(8,128)(2,1)} fusion(bf16[30,192,192]{2,1,0:T(8,128)(2,1)} %bitcast_select_fusion, s32[1024]{0:T(1024)S(1)} %pad_clamp_fusion), kind=kCustom, calls=%fused_computation.clone | custom fusion | bytes 4423800 | tf_op jit(solution)/shard_map/jit(_take)/gather | solution.py:40
  87.1 3.0 %convolution_convert_fusion.1 = bf16[30,192,192]{2,1,0:T(8,128)(2,1)S(1)} fusion(bf16[30,192,192]{2,1,0:T(8,128)(2,1)} %gather_fusion, pred[30]{0:T(512)(128)(4,1)S(1)} %compare_and_fusion, f32[192,192]{1,0:T(8,128)S(1)} %get-tuple-element.12, f32[]{:T(128)} %bitcast.7), kind=kOutput, calls=%fused_computation.6 | convolution fusion | flops 426958848 | bytes 4571170 | tf_op jit(solution)/shard_map/wab,bc->wac/dot_general | solution.py:49
  90.0 0.4 fusion.3
  90.4 0.4 fusion.2
  90.9 1.7 %collective-permute-start.2 = (bf16[192,192]{1,0:T(8,128)(2,1)S(1)}, bf16[192,192]{1,0:T(8,128)(2,1)S(1)}, u32[]{:S(2)}, u32[]{:S(2)}) collective-permute-start(bf16[192,192]{1,0:T(8,128)(2,1)S(1)} %fusion.2), channel_id=1, source_target_pairs={{0,1},{1,2},{2,3},{4,5},{5,6},{6,7},{8,9},{9,10},{10,11},{12,13},{... | collective-permute-start | bytes 221192 | tf_op jit(solution)/shard_map/ppermute | solution.py:12
  92.6 1.3 collective-permute-start.3
  93.9 3.4 %collective-permute-done.3 = bf16[192,192]{1,0:T(8,128)(2,1)S(1)} collective-permute-done((bf16[192,192]{1,0:T(8,128)(2,1)S(1)}, bf16[192,192]{1,0:T(8,128)(2,1)S(1)}, u32[]{:S(2)}, u32[]{:S(2)}) %collective-permute-start.3) | collective-permute-done | bytes 73760 | tf_op jit(solution)/shard_map/ppermute | solution.py:12
  97.3 1.0 multiply_reduce_fusion.3
  98.3 9.5 %psum.29 = f32[1]{0:T(128)} all-reduce(f32[1]{0:T(128)} %bitcast.13), channel_id=1, replica_groups=mesh['parts'=2,'seg'=4,'grp'=4] {'grp'}, use_global_device_ids=true, to_apply=%region_4.6 | all-reduce | flops 1 | bytes 8 | tf_op jit(solution)/shard_map/psum | solution.py:45
  108.5 0.7 multiply_reduce_fusion.2
  109.1 6.3 %psum.30 = f32[1]{0:T(128)} all-reduce(f32[1]{0:T(128)} %bitcast.15), channel_id=1, replica_groups=mesh['parts'=2,'seg'=4,'grp'=4] {'grp'}, use_global_device_ids=true, to_apply=%region_6.8 | all-reduce | flops 1 | bytes 8 | tf_op jit(solution)/shard_map/psum | solution.py:45
  116.1 3.0 %convolution_convert_fusion = bf16[30,192,192]{2,1,0:T(8,128)(2,1)S(1)} fusion(bf16[30,192,192]{2,1,0:T(8,128)(2,1)} %gather_fusion, pred[30]{0:T(512)(128)(4,1)S(1)} %compare_and_fusion, f32[]{:T(128)} %bitcast.16, f32[192,192]{1,0:T(8,128)S(1)} %get-tuple-element.8, f32[]{:T(128)} %bitcast.14, f32[192,192]{1,0:T(8,128)S(1)} %get-tuple-element.12, f32[]{:T(128)} %bitcast.7), kind=kOutput, calls=%fused_computation.5 | convolution fusion | flops 427069440 | bytes 4718634 | tf_op jit(solution)/shard_map/wab,bc->wac/dot_general | solution.py:49
  119.1 0.4 fusion.7
  119.5 0.4 fusion.6
  119.9 1.8 %collective-permute-start.4 = (bf16[192,192]{1,0:T(8,128)(2,1)S(1)}, bf16[192,192]{1,0:T(8,128)(2,1)S(1)}, u32[]{:S(2)}, u32[]{:S(2)}) collective-permute-start(bf16[192,192]{1,0:T(8,128)(2,1)S(1)} %fusion.6), channel_id=1, source_target_pairs={{0,1},{1,2},{2,3},{4,5},{5,6},{6,7},{8,9},{9,10},{10,11},{12,13},{... | collective-permute-start | bytes 221192 | tf_op jit(solution)/shard_map/ppermute | solution.py:12
  121.7 1.3 collective-permute-start.5
  123.0 3.4 %collective-permute-done.5 = bf16[192,192]{1,0:T(8,128)(2,1)S(1)} collective-permute-done((bf16[192,192]{1,0:T(8,128)(2,1)S(1)}, bf16[192,192]{1,0:T(8,128)(2,1)S(1)}, u32[]{:S(2)}, u32[]{:S(2)}) %collective-permute-start.5) | collective-permute-done | bytes 73760 | tf_op jit(solution)/shard_map/ppermute | solution.py:12
  126.3 1.0 multiply_reduce_fusion.1
  127.4 1.4 pad_maximum_fusion
  128.7 8.9 %psum.31 = f32[2]{0:T(128)S(1)} all-reduce(f32[2]{0:T(128)S(1)} %pad_maximum_fusion), channel_id=1, replica_groups=mesh['parts'=2,'seg'=4,'grp'=4] {'grp'}, use_global_device_ids=true, to_apply=%region_9.11 | all-reduce | flops 2 | bytes 16 | tf_op jit(solution)/shard_map/psum | solution.py:45
  137.6 0.6 fusion.27
  141.6 1.4 divide_bitcast_fusion
  (19 shorter events, 0.1 us)
Async XLA Ops:
  0.6 12.6 %copy-start = (bf16[1,1,30,192,192]{4,3,2,1,0:T(8,128)(2,1)S(1)}, bf16[1,1,30,192,192]{4,3,2,1,0:T(8,128)(2,1)}, u32[]{:S(2)}) copy-start(bf16[1,1,30,192,192]{4,3,2,1,0:T(8,128)(2,1)} %param.10) | copy-start | bytes 6635524
  0.6 78.5 %collective-permute-start = (bf16[1,1,30,192,192]{4,3,2,1,0:T(8,128)(2,1)}, bf16[1,1,30,192,192]{4,3,2,1,0:T(8,128)(2,1)}, u32[]{:S(2)}, u32[]{:S(2)}) collective-permute-start(bf16[1,1,30,192,192]{4,3,2,1,0:T(8,128)(2,1)} %param.9), channel_id=1, source_target_pairs={{0,4},{4,8},{8,12},{1,5},{5,9},{9,13},{2,6},{6,10},{10,14},{3,7},{... | collective-permute-start | bytes 6635528 | tf_op jit(solution)/shard_map/ppermute | solution.py:12
  8.4 62.9 %collective-permute-start.1 = (bf16[1,1,192,192]{3,2,1,0:T(8,128)(2,1)S(1)}, bf16[1,1,192,192]{3,2,1,0:T(8,128)(2,1)S(1)}, u32[]{:S(2)}, u32[]{:S(2)}) collective-permute-start(bf16[1,1,192,192]{3,2,1,0:T(8,128)(2,1)S(1)} %divide_convert_fusion), channel_id=1, source_target_pairs={{0,4},{4,8},{8,12},{1,5},{5,9},{9,13},{2,6},{6,10},{10,14},{3,7},{... | collective-permute-start | bytes 221192 | tf_op jit(solution)/shard_map/ppermute | solution.py:12
  15.7 55.6 %copy-start.3 = (bf16[1,1,192,192]{3,2,1,0:T(8,128)(2,1)S(1)}, bf16[1,1,192,192]{3,2,1,0:T(8,128)(2,1)}, u32[]{:S(2)}) copy-start(bf16[1,1,192,192]{3,2,1,0:T(8,128)(2,1)} %param.12) | copy-start | bytes 221188
  87.1 3.0 %copy-start.1 = (bf16[30,192,192]{2,1,0:T(8,128)(2,1)S(1)}, bf16[30,192,192]{2,1,0:T(8,128)(2,1)}, u32[]{:S(2)}) copy-start(bf16[30,192,192]{2,1,0:T(8,128)(2,1)} %broadcast_select_fusion) | copy-start | bytes 6635524
  90.9 3.0 %collective-permute-start.2 = (bf16[192,192]{1,0:T(8,128)(2,1)S(1)}, bf16[192,192]{1,0:T(8,128)(2,1)S(1)}, u32[]{:S(2)}, u32[]{:S(2)}) collective-permute-start(bf16[192,192]{1,0:T(8,128)(2,1)S(1)} %fusion.2), channel_id=1, source_target_pairs={{0,1},{1,2},{2,3},{4,5},{5,6},{6,7},{8,9},{9,10},{10,11},{12,13},{... | collective-permute-start | bytes 221192 | tf_op jit(solution)/shard_map/ppermute | solution.py:12
  92.6 4.7 %collective-permute-start.3 = (bf16[192,192]{1,0:T(8,128)(2,1)S(1)}, bf16[192,192]{1,0:T(8,128)(2,1)S(1)}, u32[]{:S(2)}, u32[]{:S(2)}) collective-permute-start(bf16[192,192]{1,0:T(8,128)(2,1)S(1)} %fusion.3), channel_id=1, source_target_pairs={{1,0},{2,1},{3,2},{5,4},{6,5},{7,6},{9,8},{10,9},{11,10},{13,12},{... | collective-permute-start | bytes 221192 | tf_op jit(solution)/shard_map/ppermute | solution.py:12
  116.1 3.0 %copy-start.2 = (bf16[30,192,192]{2,1,0:T(8,128)(2,1)S(1)}, bf16[30,192,192]{2,1,0:T(8,128)(2,1)}, u32[]{:S(2)}) copy-start(bf16[30,192,192]{2,1,0:T(8,128)(2,1)} %broadcast_select_fusion) | copy-start | bytes 6635524
  119.9 3.1 %collective-permute-start.4 = (bf16[192,192]{1,0:T(8,128)(2,1)S(1)}, bf16[192,192]{1,0:T(8,128)(2,1)S(1)}, u32[]{:S(2)}, u32[]{:S(2)}) collective-permute-start(bf16[192,192]{1,0:T(8,128)(2,1)S(1)} %fusion.6), channel_id=1, source_target_pairs={{0,1},{1,2},{2,3},{4,5},{5,6},{6,7},{8,9},{9,10},{10,11},{12,13},{... | collective-permute-start | bytes 221192 | tf_op jit(solution)/shard_map/ppermute | solution.py:12
  121.7 4.7 %collective-permute-start.5 = (bf16[192,192]{1,0:T(8,128)(2,1)S(1)}, bf16[192,192]{1,0:T(8,128)(2,1)S(1)}, u32[]{:S(2)}, u32[]{:S(2)}) collective-permute-start(bf16[192,192]{1,0:T(8,128)(2,1)S(1)} %fusion.7), channel_id=1, source_target_pairs={{1,0},{2,1},{3,2},{5,4},{6,5},{7,6},{9,8},{10,9},{11,10},{13,12},{... | collective-permute-start | bytes 221192 | tf_op jit(solution)/shard_map/ppermute | solution.py:12
where the time goes:
time: 145 us; the launch traced here: 144 us
  waiting for transfers between devices  58.5 us (40%)
  blocking collectives  30.9 us (21%)
  starting transfers between devices  14.8 us (10%)
  other arithmetic  14.3 us (10%)
  matrix products  10.4 us (7%)
  between operations  8.05 us (6%)
  local copies, waits for them, and re-layouts  7.21 us (5%)
    ppermute x6, waiting for transfers between devices, from_behind(): return lax.ppermute(block, axis, route)  58.5 us
    psum x4, blocking collectives, grp_means(): return lax.psum(jnp.stack(values), 'grp') / entry_count  30.9 us
    ppermute x6, starting transfers between devices, from_behind(): return lax.ppermute(block, axis, route)  14.8 us
    dot_general x2, matrix products, matvec(): jnp.einsum('wab,bc->wac', left_sorted, rounded, preferred_element_type=jn...  5.91 us
    gather x1, local copies, waits for them, and re-layouts, body(): left_sorted = jnp.take(left_env, ordering, axis=0)  4.18 us
    select_n x1, other arithmetic, body(): right_sorted = jnp.take(env_right[0, 0], ordering, axis=0)  3.86 us
    select_n x1, other arithmetic, body(): left_env = jnp.where(first_seg, vacuum, got_env[0, 0])  3.76 us
    dot_general x6, matrix products, matvec(): jnp.einsum('wac,wcd->ad', inner_prod[lo:hi], right_sorted[lo:hi], preferr...  3.68 us
  transfers between devices with their start and end apart: 6, of which 3 were waited for; matrix products, arithmetic and copies ran while one was open for 7% of the time, Pallas kernels for 0%

commit v1 on v0

v1 whole, which is shorter than its diff:
```python
import functools

import jax
import jax.numpy as jnp
from jax import lax
from jax.experimental import pallas as pl
from jax.experimental.pallas import tpu as pltpu
from jax.sharding import PartitionSpec as P

eps_value = 1e-06
lanes = 128
f32 = jnp.float32
bf16 = jnp.bfloat16


def pack(dst, x):
    size = x.shape[0]
    half, rest = size // 2, size - lanes
    dst[0:size, :] = x[:, :lanes]
    dst[size : size + half, :] = jnp.concatenate([x[:half, lanes:], x[half:, lanes:]], axis=1)


def unpack(src, size):
    half, rest = size // 2, size - lanes
    tail = src[size : size + half, :]
    tall = jnp.concatenate([tail[:, :rest], tail[:, rest:]], axis=0)
    return jnp.concatenate([src[0:size, :], tall], axis=1)


def kernel(
    segs, grps, chunk,
    el, er, sl, sr, bw, chg, rows,
    theta_out, energy_out,
    elv, erv, send_a, send_b, recv_a, recv_b, full_a, full_b,
    site_send, site_recv, ch_loc, ch_rem,
    theta, v16, image, acc,
    slab_send, slab_recv, z_send, z_recv, res_send, res_recv,
    stat_send, stat_recv, low_send, low_recv,
    loc_sem, env_s, env_r, site_s, site_r, slab_s, slab_r,
    z_s, z_r, res_s, res_r, stat_s, stat_r, low_s, low_r,
):
    width, size, _ = el.shape
    half = width // 2
    chunks = half // chunk
    entry_count = float(grps * size * size)
    s = lax.axis_index("seg")
    q = lax.axis_index("grp")
    has_up = s < segs - 1
    has_dn = s > 0
    has_hi = q < grps - 1
    has_lo = q > 0
    up, dn = jnp.minimum(s + 1, segs - 1), jnp.maximum(s - 1, 0)
    hi, lo = jnp.minimum(q + 1, grps - 1), jnp.maximum(q - 1, 0)
    upper, lower = 0, 1

    def remote(src, dst, ssem, rsem, **where):
        return pltpu.make_async_remote_copy(
            src_ref=src, dst_ref=dst, send_sem=ssem, recv_sem=rsem,
            device_id=where, device_id_type=pl.DeviceIdType.MESH,
        )

    def load_a(k):
        at = pl.ds(k * chunk, chunk)
        return pltpu.make_async_copy(el.at[at], elv.at[at], loc_sem.at[k])

    def load_b(k):
        at = pl.ds(half + k * chunk, chunk)
        return pltpu.make_async_copy(er.at[at], erv.at[at], loc_sem.at[chunks + k])

    def load_rest_a():
        at = pl.ds(half, half)
        return pltpu.make_async_copy(el.at[at], elv.at[at], loc_sem.at[2 * chunks])

    def load_rest_b():
        at = pl.ds(0, half)
        return pltpu.make_async_copy(er.at[at], erv.at[at], loc_sem.at[2 * chunks + 1])

    for k in range(chunks):
        load_a(k).start()
        load_b(k).start()
    load_rest_a().start()
    load_rest_b().start()

    barrier = pltpu.get_barrier_semaphore()
    for d in range(1, grps):
        pl.semaphore_signal(
            barrier, inc=1, device_id={"grp": lax.rem(q + d, grps)},
            device_id_type=pl.DeviceIdType.MESH)

    @pl.when(has_up)
    def _():
        for j in range(grps):
            pl.semaphore_signal(
                barrier, inc=1, device_id={"seg": up, "grp": j},
                device_id_type=pl.DeviceIdType.MESH)

    @pl.when(has_dn)
    def _():
        for j in range(grps):
            pl.semaphore_signal(
                barrier, inc=1, device_id={"seg": dn, "grp": j},
                device_id_type=pl.DeviceIdType.MESH)

    scaled = (sl[...].astype(f32) / bw[...]).astype(bf16)
    site_right = sr[...]
    pack(site_send.at[0], scaled)
    pack(site_send.at[1], site_right)
    for w in range(width):
        ch_loc[w : w + 1, :] = jnp.full((1, size), chg[0, w], jnp.int32).astype(f32)
    pad = ch_loc.shape[0] - width
    ch_loc[width:, :] = jnp.full((pad, size), rows[0, 0], jnp.int32).astype(f32)

    pl.semaphore_wait(
        barrier, grps - 1 + grps * (has_up.astype(jnp.int32) + has_dn.astype(jnp.int32)))

    def site_up():
        return remote(site_send.at[0], site_recv.at[0], site_s.at[0], site_r.at[0], seg=up)

    def site_dn():
        return remote(site_send.at[1], site_recv.at[1], site_s.at[1], site_r.at[1], seg=dn)

    def ch_dn():
        return remote(ch_loc, ch_rem, site_s.at[2], site_r.at[2], seg=dn)

    def env_up(k):
        return remote(send_a.at[k], recv_a.at[k], env_s.at[0, k], env_r.at[0, k], seg=up)

    def env_dn(k):
        return remote(send_b.at[k], recv_b.at[k], env_s.at[1, k], env_r.at[1, k], seg=dn)

    @pl.when(has_up)
    def _():
        site_up().start()

    @pl.when(has_dn)
    def _():
        site_dn().start()
        ch_dn().start()

    def send_chunk(k, carry):
        load_a(k).wait()
        load_b(k).wait()

        @pl.when(has_up)
        def _():
            for j in range(chunk):
                pack(send_a.at[k, j], elv[k * chunk + j])
            env_up(k).start()

        @pl.when(has_dn)
        def _():
            for j in range(chunk):
                pack(send_b.at[k, j], erv[half + k * chunk + j])
            env_dn(k).start()

        return carry

    lax.fori_loop(0, chunks, send_chunk, 0)
    load_rest_a().wait()
    load_rest_b().wait()

    row_at = lax.broadcasted_iota(jnp.int32, (size, size), 0)
    col_at = lax.broadcasted_iota(jnp.int32, (size, size), 1)
    eye_block = jnp.where(row_at == col_at, 1.0, 0.0)

    @pl.when(jnp.logical_not(has_dn))
    def _():
        for w in range(half):
            full_a[w] = (eye_block if w == 0 else jnp.zeros_like(eye_block)).astype(bf16)

    row_f = row_at.astype(f32)

    def live(ch):
        return jnp.where(row_f < ch[width : width + 1, :], 1.0, 0.0)

    @pl.when(has_dn)
    def _():
        site_up().wait_recv()
        edge = unpack(site_recv.at[0], size)
        theta[upper] = jnp.dot(edge, site_right, preferred_element_type=f32) * live(ch_loc)

    @pl.when(jnp.logical_not(has_dn))
    def _():
        theta[upper] = site_right.astype(f32) * live(ch_loc)

    @pl.when(has_up)
    def _():
        site_dn().wait_recv()
        ch_dn().wait_recv()
        above = unpack(site_recv.at[1], size)
        theta[lower] = jnp.dot(scaled, above, preferred_element_type=f32) * live(ch_rem)

    @pl.when(jnp.logical_not(has_up))
    def _():
        theta[lower] = jnp.zeros((size, size), f32)

    def column_sums(x):
        return jnp.sum(x, axis=0, keepdims=True)

    def stat_copy(slot, d):
        return remote(
            stat_send.at[slot], stat_recv.at[slot, q], stat_s.at[slot, d], stat_r.at[slot, d],
            grp=lax.rem(q + d, grps))

    def stat_tile(values):
        at = lax.broadcasted_iota(jnp.int32, (8, size), 0)
        tile = jnp.zeros((8, size), f32)
        for i, value in enumerate(values):
            tile = jnp.where(at == i, value, tile)
        return tile

    def stat_start(slot, values):
        tile = stat_tile(values)
        stat_send[slot] = tile
        stat_recv[slot, q] = tile
        for d in range(1, grps):
            stat_copy(slot, d).start()

    def total(tiles, extra=None):
        tile = tiles[0]
        for j in range(1, grps):
            tile = tile + tiles[j]
        if extra is not None:
            for j in range(grps):
                tile = tile + extra[j]
        return jnp.sum(tile, axis=1, keepdims=True) / entry_count

    def stat_finish(slot):
        for d in range(1, grps):
            stat_copy(slot, d).wait_recv()
        return stat_recv.at[slot]

    stat_start(0, [column_sums(theta[i] * theta[i]) for i in (upper, lower)])
    norms = total(stat_finish(0))
    for i in (upper, lower):
        basis = theta[i] / jnp.sqrt(norms[i : i + 1, :] + eps_value)
        theta[i] = basis
        v16[i] = basis.astype(bf16)
        acc[i] = jnp.zeros(acc.shape[1:], f32)

    def one_term(a, v, ch_row, b):
        inner = jnp.dot(a, v, preferred_element_type=f32).astype(bf16)
        parts = [inner * jnp.where(ch_row == c, 1.0, 0.0).astype(bf16) for c in (-1.0, 0.0, 1.0)]
        return jnp.dot(jnp.concatenate(parts, axis=0), b, preferred_element_type=f32)

    def upper_chunk(k):
        value = None
        for j in range(chunk):
            w = k * chunk + j
            term = one_term(full_a[w], v16[upper], ch_loc[pl.ds(w, 1), :], erv[w])
            value = term if value is None else value + term
        acc[upper] = acc[upper] + value

    def lower_chunk(k):
        value = None
        for j in range(chunk):
            w = k * chunk + j
            term = one_term(elv[half + w], v16[lower], ch_rem[pl.ds(half + w, 1), :], full_b[w])
            value = term if value is None else value + term
        acc[lower] = acc[lower] + value

    def first_chunk(k, carry):
        @pl.when(has_dn)
        def _():
            env_up(k).wait_recv()
            for j in range(chunk):
                full_a[k * chunk + j] = unpack(recv_a.at[k, j], size)

        upper_chunk(k)

        @pl.when(has_up)
        def _():
            env_dn(k).wait_recv()
            for j in range(chunk):
                full_b[k * chunk + j] = unpack(recv_b.at[k, j], size)
            lower_chunk(k)

        return carry

    lax.fori_loop(0, chunks, first_chunk, 0)

    def slab_copy(role, way):
        return remote(
            slab_send.at[role, way], slab_recv.at[role, way], slab_s.at[role, way],
            slab_r.at[role, way], grp=(lo, hi)[way])

    def res_copy(role, way):
        return remote(
            res_send.at[role], res_recv.at[role, way], res_s.at[role, way],
            res_r.at[role, way], grp=(lo, hi)[way])

    def z_copy(role):
        return remote(
            z_send.at[role], z_recv.at[1 - role], z_s.at[role], z_r.at[1 - role],
            seg=(dn, up)[role])

    def z_incoming(role):
        return remote(
            z_send.at[role], z_recv.at[role], z_s.at[role], z_r.at[role],
            seg=(dn, up)[role])

    def slab(role, c):
        return acc[role, c * size : (c + 1) * size, :]

    def send_slabs(role):
        @pl.when(has_lo)
        def _():
            pack(slab_send.at[role, 0], slab(role, 0).astype(bf16))
            slab_copy(role, 0).start()

        @pl.when(has_hi)
        def _():
            pack(slab_send.at[role, 1], slab(role, 2).astype(bf16))
            slab_copy(role, 1).start()

    def join_slabs(role, ch):
        image[role] = slab(role, 1).astype(bf16).astype(f32)

        @pl.when(has_hi)
        def _():
            slab_copy(role, 0).wait_recv()
            image[role] = image[role] + unpack(slab_recv.at[role, 0], size).astype(f32)

        @pl.when(has_lo)
        def _():
            slab_copy(role, 1).wait_recv()
            image[role] = image[role] + unpack(slab_recv.at[role, 1], size).astype(f32)

        half_image = (image[role] * live(ch)).astype(bf16)
        pack(z_send.at[role], half_image)
        z_copy(role).start()
        image[role] = half_image.astype(f32)

    send_slabs(upper)

    @pl.when(has_up)
    def _():
        send_slabs(lower)

    @pl.when(has_dn)
    def _():
        join_slabs(upper, ch_loc)

    @pl.when(jnp.logical_not(has_dn))
    def _():
        image[upper] = slab(upper, 1).astype(bf16).astype(f32)

        @pl.when(has_hi)
        def _():
            slab_copy(upper, 0).wait_recv()
            image[upper] = image[upper] + unpack(slab_recv.at[upper, 0], size).astype(f32)

        @pl.when(has_lo)
        def _():
            slab_copy(upper, 1).wait_recv()
            image[upper] = image[upper] + unpack(slab_recv.at[upper, 1], size).astype(f32)

        image[upper] = image[upper] * live(ch_loc)

    @pl.when(has_up)
    def _():
        join_slabs(lower, ch_rem)

    @pl.when(jnp.logical_not(has_up))
    def _():
        image[lower] = jnp.zeros((size, size), f32)

    @pl.when(has_dn)
    def _():
        z_incoming(upper).wait_recv()
        image[upper] = image[upper] + unpack(z_recv.at[upper], size).astype(f32)

    @pl.when(has_up)
    def _():
        z_incoming(lower).wait_recv()
        image[lower] = image[lower] + unpack(z_recv.at[lower], size).astype(f32)

    stat_start(1, [column_sums(theta[i] * image[i]) for i in (upper, lower)])
    diags = total(stat_finish(1))
    diag_one = diags[0:1, :]

    def send_res(role):
        residual = image[role] - diags[role : role + 1, :] * theta[role]
        rounded = residual.astype(bf16)
        v16[role] = rounded
        pack(res_send.at[role], rounded)

        @pl.when(has_lo)
        def _():
            res_copy(role, 0).start()

        @pl.when(has_hi)
        def _():
            res_copy(role, 1).start()

        return residual

    residual = send_res(upper)

    @pl.when(has_up)
    def _():
        send_res(lower)

    for i in (upper, lower):
        acc[i] = jnp.zeros(acc.shape[1:], f32)

    def second_chunk(k, carry):
        upper_chunk(k)

        @pl.when(has_up)
        def _():
            lower_chunk(k)

        return carry

    lax.fori_loop(0, chunks, second_chunk, 0)

    def overlap(role, own):
        theta_out[...] = own * slab(role, 1)

        @pl.when(has_hi)
        def _():
            res_copy(role, 0).wait_recv()
            above = unpack(res_recv.at[role, 0], size).astype(f32)
            theta_out[...] = theta_out[...] + above * slab(role, 2)

        @pl.when(has_lo)
        def _():
            res_copy(role, 1).wait_recv()
            below = unpack(res_recv.at[role, 1], size).astype(f32)
            theta_out[...] = theta_out[...] + below * slab(role, 0)

        return column_sums(theta_out[...])

    def low_copy(j):
        return remote(
            low_send, low_recv.at[q], low_s.at[j], low_r.at[q], seg=up, grp=j)

    def low_incoming(j):
        return remote(low_send, low_recv.at[j], low_s.at[j], low_r.at[j], seg=dn, grp=j)

    @pl.when(has_up)
    def _():
        zero = jnp.zeros((1, size), f32)
        low_send[...] = stat_tile([zero, zero, overlap(lower, v16[lower].astype(f32))])
        for j in range(grps):
            low_copy(j).start()

    stat_start(
        2,
        [
            column_sums(residual * residual),
            column_sums(residual * image[upper]),
            overlap(upper, residual),
        ],
    )

    @pl.when(has_dn)
    def _():
        for j in range(grps):
            low_incoming(j).wait_recv()

    @pl.when(jnp.logical_not(has_dn))
    def _():
        low_recv[...] = jnp.zeros(low_recv.shape, f32)

    sums = total(stat_finish(2), low_recv)
    scale = 1.0 / jnp.sqrt(sums[0:1, :] + eps_value)
    coupling = sums[1:2, :] * scale
    diag_two = sums[2:3, :] * scale * scale
    half_gap = 0.5 * (diag_one - diag_two)
    energy = 0.5 * (diag_one + diag_two) - jnp.sqrt(half_gap * half_gap + coupling * coupling)
    lead_coef = diag_two - energy
    norm_scale = jnp.sqrt(lead_coef * lead_coef + coupling * coupling)
    energy_out[...] = energy
    theta_out[...] = (lead_coef * theta[upper] - coupling * (residual * scale)) / norm_scale

    @pl.when(has_up)
    def _():
        site_up().wait_send()
        z_copy(lower).wait_send()
        for k in range(chunks):
            env_up(k).wait_send()
        for j in range(grps):
            low_copy(j).wait_send()

    @pl.when(has_dn)
    def _():
        site_dn().wait_send()
        ch_dn().wait_send()
        z_copy(upper).wait_send()
        for k in range(chunks):
            env_dn(k).wait_send()

    for slot in range(3):
        for d in range(1, grps):
            stat_copy(slot, d).wait_send()

    def drain(role):
        @pl.when(has_lo)
        def _():
            slab_copy(role, 0).wait_send()
            res_copy(role, 0).wait_send()

        @pl.when(has_hi)
        def _():
            slab_copy(role, 1).wait_send()
            res_copy(role, 1).wait_send()

    drain(upper)

    @pl.when(has_up)
    def _():
        drain(lower)


def body(env_left, env_right, site_left, site_right, bond_weights, mpo_charge, sector_rows):
    width, size = env_left.shape[2:4]
    segs, grps = lax.axis_size("seg"), lax.axis_size("grp")
    half = width // 2
    chunk = 3 if half % 3 == 0 else 1
    chunks = half // chunk
    tall = size + size // 2
    charge_rows = (width // 8 + 1) * 8
    vmem = pl.BlockSpec(memory_space=pltpu.VMEM)
    smem = pl.BlockSpec(memory_space=pltpu.SMEM)
    hbm = pl.BlockSpec(memory_space=pl.ANY)
    dma = pltpu.SemaphoreType.DMA
    theta_new, energy = pl.pallas_call(
        functools.partial(kernel, segs, grps, chunk),
        out_shape=(
            jax.ShapeDtypeStruct((size, size), f32),
            jax.ShapeDtypeStruct((1, 1), f32),
        ),
        in_specs=[hbm, hbm, vmem, vmem, vmem, smem, smem],
        out_specs=(vmem, vmem),
        scratch_shapes=[
            pltpu.VMEM((width, size, size), bf16),
            pltpu.VMEM((width, size, size), bf16),
            pltpu.VMEM((chunks, chunk, tall, lanes), bf16),
            pltpu.VMEM((chunks, chunk, tall, lanes), bf16),
            pltpu.VMEM((chunks, chunk, tall, lanes), bf16),
            pltpu.VMEM((chunks, chunk, tall, lanes), bf16),
            pltpu.VMEM((half, size, size), bf16),
            pltpu.VMEM((half, size, size), bf16),
            pltpu.VMEM((2, tall, lanes), bf16),
            pltpu.VMEM((2, tall, lanes), bf16),
            pltpu.VMEM((charge_rows, size), f32),
            pltpu.VMEM((charge_rows, size), f32),
            pltpu.VMEM((2, size, size), f32),
            pltpu.VMEM((2, size, size), bf16),
            pltpu.VMEM((2, size, size), f32),
            pltpu.VMEM((2, 3 * size, size), f32),
            pltpu.VMEM((2, 2, tall, lanes), bf16),
            pltpu.VMEM((2, 2, tall, lanes), bf16),
            pltpu.VMEM((2, tall, lanes), bf16),
            pltpu.VMEM((2, tall, lanes), bf16),
            pltpu.VMEM((2, tall, lanes), bf16),
            pltpu.VMEM((2, 2, tall, lanes), bf16),
            pltpu.VMEM((3, 8, size), f32),
            pltpu.VMEM((3, grps, 8, size), f32),
            pltpu.VMEM((8, size), f32),
            pltpu.VMEM((grps, 8, size), f32),
            dma((2 * chunks + 2,)),
            dma((2, chunks)),
            dma((2, chunks)),
            dma((3,)),
            dma((3,)),
            dma((2, 2)),
            dma((2, 2)),
            dma((2,)),
            dma((2,)),
            dma((2, 2)),
            dma((2, 2)),
            dma((3, grps)),
            dma((3, grps)),
            dma((grps,)),
            dma((grps,)),
        ],
        compiler_params=pltpu.CompilerParams(
            collective_id=0, has_side_effects=True, vmem_limit_bytes=40 * 1024 * 1024
        ),
        cost_estimate=pl.CostEstimate(
            flops=16 * width * size**3, bytes_accessed=4 * width * size * size, transcendentals=0
        ),
    )(
        env_left[0, 0],
        env_right[0, 0],
        site_left[0, 0],
        site_right[0, 0],
        bond_weights[0],
        mpo_charge,
        sector_rows,
    )
    return (theta_new[None, None], energy[0])


def solution(mesh):
    return jax.shard_map(
        body,
        mesh=mesh,
        in_specs=(
            P(("parts", "seg"), "grp", None, None, None),
            P(("parts", "seg"), "grp", None, None, None),
            P(("parts", "seg"), "grp", None, None),
            P(("parts", "seg"), "grp", None, None),
            P(("parts", "seg"), "grp", None),
            P(("parts", "seg"), None),
            P(("parts", "seg"), "grp"),
        ),
        out_specs=(P(("parts", "seg"), "grp", None, None), P(("parts", "seg"))),
        check_vma=False,
    )
```

time: 145 us -> 67 us (0.46)
  waiting for transfers between devices: 58.5 us -> 0 us
  Pallas kernels: 0 us -> 56.2 us
  blocking collectives: 30.9 us -> 0 us
  starting transfers between devices: 14.8 us -> 0 us
  other arithmetic: 14.3 us -> 0 us
  matrix products: 10.4 us -> 0 us
  between operations: 8.05 us -> 3.12 us
    ppermute x6 -> x0, waiting for transfers between devices: 58.5 us -> none  [from_behind(): return lax.ppermute(block, axis, route)]
    pallas_call x0 -> x1, Pallas kernels: none -> 56.2 us  [body(): pl.pallas_call(functools.partial(kernel, segs, grps, chunk), out_shape=(j...]
    psum x4 -> x0, blocking collectives: 30.9 us -> none  [grp_means(): return lax.psum(jnp.stack(values), 'grp') / entry_count]
    ppermute x6 -> x0, starting transfers between devices: 14.8 us -> none  [from_behind(): return lax.ppermute(block, axis, route)]
    dot_general x9 -> x0, matrix products: 10.4 us -> none  [the longest x2 5.91 us: matvec(): jnp.einsum('wab,bc->wac', left_sorted, rounded, preferred_element_type=jn...]
    select_n x3 -> x0, other arithmetic: 7.63 us -> none  [the longest x1 3.86 us: body(): right_sorted = jnp.take(env_right[0, 0], ordering, axis=0)]
    unnamed x8 -> x13, local copies, waits for them, and re-layouts: 0.02 us -> 7.46 us
    gather x2 -> x0, local copies, waits for them, and re-layouts: 6.59 us -> none  [the longest x1 4.18 us: body(): left_sorted = jnp.take(left_env, ordering, axis=0)]
  transfers between devices with their start and end apart: 6 -> 0, of which waited for: 3 -> 0; matrix products, arithmetic and copies ran while one was open for 7% -> 0% of each run, Pallas kernels for 0% -> 0%
where the time goes in v1:
time: 67 us; the launch traced here: 66.7 us
  Pallas kernels  56.2 us (84%)
  local copies, waits for them, and re-layouts  7.46 us (11%)
  between operations  3.12 us (5%)
    pallas_call x1, Pallas kernels, body(): pl.pallas_call(functools.partial(kernel, segs, grps, chunk), out_shape=(j...  56.2 us
    unnamed x13, local copies, waits for them, and re-layouts  7.46 us

profile of v1, /device:TPU:0, one launch (start us, length us, event | category | flops | bytes accessed | tf_op | source)
XLA Modules:
  0.0 66.7 jit_solution(13398337589123051794)
XLA Ops:
  1.3 0.0 copy-start
  1.3 1.8 %copy-done = bf16[1,1,30,192,192]{4,3,2,1,0:T(8,128)(2,1)S(1)} copy-done((bf16[1,1,30,192,192]{4,3,2,1,0:T(8,128)(2,1)S(1)}, bf16[1,1,30,192,192]{4,3,2,1,0:T(8,128)(2,1)}, u32[]{:S(2)}) %copy-start) | copy-done | bytes 2211864
  3.1 0.0 copy-start.1
  3.1 1.8 %copy-done.1 = bf16[1,1,30,192,192]{4,3,2,1,0:T(8,128)(2,1)S(1)} copy-done((bf16[1,1,30,192,192]{4,3,2,1,0:T(8,128)(2,1)S(1)}, bf16[1,1,30,192,192]{4,3,2,1,0:T(8,128)(2,1)}, u32[]{:S(2)}) %copy-start.1) | copy-done | bytes 2211864
  4.9 0.0 copy-start.2
  4.9 0.9 %copy-done.2 = bf16[1,1,192,192]{3,2,1,0:T(8,128)(2,1)S(1)} copy-done((bf16[1,1,192,192]{3,2,1,0:T(8,128)(2,1)S(1)}, bf16[1,1,192,192]{3,2,1,0:T(8,128)(2,1)}, u32[]{:S(2)}) %copy-start.2) | copy-done | bytes 73752
  5.8 0.0 copy-start.3
  5.8 0.9 %copy-done.3 = bf16[1,1,192,192]{3,2,1,0:T(8,128)(2,1)S(1)} copy-done((bf16[1,1,192,192]{3,2,1,0:T(8,128)(2,1)S(1)}, bf16[1,1,192,192]{3,2,1,0:T(8,128)(2,1)}, u32[]{:S(2)}) %copy-start.3) | copy-done | bytes 73752
  6.7 0.0 copy-start.4
  6.7 0.7 %copy-done.4 = f32[1,1,192]{2,1,0:T(1,128)S(1)} copy-done((f32[1,1,192]{2,1,0:T(1,128)S(1)}, f32[1,1,192]{2,1,0:T(1,128)}, u32[]{:S(2)}) %copy-start.4) | copy-done | bytes 792
  7.4 0.0 copy-start.5
  7.4 0.7 copy-done.5
  8.1 56.2 %shard_map.86 = (f32[192,192]{1,0:T(8,128)S(1)}, f32[1,1]{1,0:T(1,128)}) custom-call(bf16[30,192,192]{2,1,0:T(8,128)(2,1)S(1)} %bitcast.8, bf16[30,192,192]{2,1,0:T(8,128)(2,1)S(1)} %bitcast.9, bf16[192,192]{1,0:T(8,128)(2,1)S(1)} %bitcast.10, bf16[192,192]{1,0:T(8,128)(2,1)S(1)} %bitcast.11, f32[1,192]{1,0:T(1,128)S(1)} %bitcast.12, s32[1,30]{1,0:T(1,128)S(1)} %copy-done.5, ...), custom_call_target="tpu_custom_call" | custom-call | flops 3397386240 | bytes 4423680 | tf_op jit(solution)/shard_map/pallas_call | solution.py:529
  64.2 0.7 %copy.12 = f32[1,1,192,192]{3,2,1,0:T(8,128)} copy(f32[1,1,192,192]{3,2,1,0:T(8,128)S(1)} %bitcast.7) | data formatting | bytes 294912
Async XLA Ops:
  1.3 1.8 %copy-start = (bf16[1,1,30,192,192]{4,3,2,1,0:T(8,128)(2,1)S(1)}, bf16[1,1,30,192,192]{4,3,2,1,0:T(8,128)(2,1)}, u32[]{:S(2)}) copy-start(bf16[1,1,30,192,192]{4,3,2,1,0:T(8,128)(2,1)} %param.7) | copy-start | bytes 6635524
  3.1 1.8 %copy-start.1 = (bf16[1,1,30,192,192]{4,3,2,1,0:T(8,128)(2,1)S(1)}, bf16[1,1,30,192,192]{4,3,2,1,0:T(8,128)(2,1)}, u32[]{:S(2)}) copy-start(bf16[1,1,30,192,192]{4,3,2,1,0:T(8,128)(2,1)} %param.8) | copy-start | bytes 6635524
  4.9 0.9 %copy-start.2 = (bf16[1,1,192,192]{3,2,1,0:T(8,128)(2,1)S(1)}, bf16[1,1,192,192]{3,2,1,0:T(8,128)(2,1)}, u32[]{:S(2)}) copy-start(bf16[1,1,192,192]{3,2,1,0:T(8,128)(2,1)} %param.9) | copy-start | bytes 221188
  5.8 0.9 %copy-start.3 = (bf16[1,1,192,192]{3,2,1,0:T(8,128)(2,1)S(1)}, bf16[1,1,192,192]{3,2,1,0:T(8,128)(2,1)}, u32[]{:S(2)}) copy-start(bf16[1,1,192,192]{3,2,1,0:T(8,128)(2,1)} %param.10) | copy-start | bytes 221188
  6.7 0.7 %copy-start.4 = (f32[1,1,192]{2,1,0:T(1,128)S(1)}, f32[1,1,192]{2,1,0:T(1,128)}, u32[]{:S(2)}) copy-start(f32[1,1,192]{2,1,0:T(1,128)} %param.11) | copy-start | bytes 2308
  7.4 0.7 copy-start.5

commit v2 on v1

--- a/solution.py
+++ b/solution.py
@@ -29,9 +29,9 @@
 
 def kernel(
     segs, grps, chunk,
-    el, er, sl, sr, bw, chg, rows,
+    el, er, sl_in, sr_in, bw_in, chg_in, rows_in,
     theta_out, energy_out,
-    elv, erv, send_a, send_b, recv_a, recv_b, full_a, full_b,
+    sl, sr, bw, chg, rows, elv, erv, send_a, send_b, recv_a, recv_b, full_a, full_b,
     site_send, site_recv, ch_loc, ch_rem,
     theta, v16, image, acc,
     slab_send, slab_recv, z_send, z_recv, res_send, res_recv,
@@ -75,6 +75,13 @@
         at = pl.ds(0, half)
         return pltpu.make_async_copy(er.at[at], erv.at[at], loc_sem.at[2 * chunks + 1])
 
+    small = [
+        pltpu.make_async_copy(src, dst, loc_sem.at[2 * chunks + 2 + i])
+        for i, (src, dst) in enumerate(
+            ((sl_in, sl), (bw_in, bw), (sr_in, sr), (chg_in, chg), (rows_in, rows)))
+    ]
+    for copy in small:
+        copy.start()
     for k in range(chunks):
         load_a(k).start()
         load_b(k).start()
@@ -101,6 +108,8 @@
                 barrier, inc=1, device_id={"seg": dn, "grp": j},
                 device_id_type=pl.DeviceIdType.MESH)
 
+    for copy in small:
+        copy.wait()
     scaled = (sl[...].astype(f32) / bw[...]).astype(bf16)
     site_right = sr[...]
     pack(site_send.at[0], scaled)
@@ -523,8 +532,7 @@
     tall = size + size // 2
     charge_rows = (width // 8 + 1) * 8
     vmem = pl.BlockSpec(memory_space=pltpu.VMEM)
-    smem = pl.BlockSpec(memory_space=pltpu.SMEM)
-    hbm = pl.BlockSpec(memory_space=pl.ANY)
+    hbm = pl.BlockSpec(memory_space=pltpu.HBM)
     dma = pltpu.SemaphoreType.DMA
     theta_new, energy = pl.pallas_call(
         functools.partial(kernel, segs, grps, chunk),
@@ -532,9 +540,14 @@
             jax.ShapeDtypeStruct((size, size), f32),
             jax.ShapeDtypeStruct((1, 1), f32),
         ),
-        in_specs=[hbm, hbm, vmem, vmem, vmem, smem, smem],
+        in_specs=[hbm] * 7,
         out_specs=(vmem, vmem),
         scratch_shapes=[
+            pltpu.VMEM((size, size), bf16),
+            pltpu.VMEM((size, size), bf16),
+            pltpu.VMEM((1, size), f32),
+            pltpu.SMEM(mpo_charge.shape, jnp.int32),
+            pltpu.SMEM(sector_rows.shape, jnp.int32),
             pltpu.VMEM((width, size, size), bf16),
             pltpu.VMEM((width, size, size), bf16),
             pltpu.VMEM((chunks, chunk, tall, lanes), bf16),
@@ -561,7 +574,7 @@
             pltpu.VMEM((3, grps, 8, size), f32),
             pltpu.VMEM((8, size), f32),
             pltpu.VMEM((grps, 8, size), f32),
-            dma((2 * chunks + 2,)),
+            dma((2 * chunks + 7,)),
             dma((2, chunks)),
             dma((2, chunks)),
             dma((3,)),
@@ -578,7 +591,7 @@
             dma((grps,)),
         ],
         compiler_params=pltpu.CompilerParams(
-            collective_id=0, has_side_effects=True, vmem_limit_bytes=40 * 1024 * 1024
+            collective_id=0, has_side_effects=True, vmem_limit_bytes=62 * 1024 * 1024
         ),
         cost_estimate=pl.CostEstimate(
             flops=16 * width * size**3, bytes_accessed=4 * width * size * size, transcendentals=0

time: 67 us -> 59.4 us (0.89)
  local copies, waits for them, and re-layouts: 7.46 us -> 1.62 us
  Pallas kernels: 56.2 us -> 54.6 us
    unnamed x13 -> x1, local copies, waits for them, and re-layouts: 7.46 us -> 1.62 us
    pallas_call x1, Pallas kernels: 56.2 us -> 54.6 us  [body(): pl.pallas_call(functools.partial(kernel, segs, grps, chunk), out_shape=(j...]
where the time goes in v2:
time: 59.4 us; the launch traced here: 59.2 us
  Pallas kernels  54.6 us (92%)
  between operations  3.05 us (5%)
  local copies, waits for them, and re-layouts  1.62 us (3%)
    pallas_call x1, Pallas kernels, body(): pl.pallas_call(functools.partial(kernel, segs, grps, chunk), out_shape=(j...  54.6 us
    unnamed x1, local copies, waits for them, and re-layouts  1.62 us

profile of v2, /device:TPU:0, one launch (start us, length us, event | category | flops | bytes accessed | tf_op | source)
XLA Modules:
  0.0 59.2 jit_solution(17590174746341629200)
XLA Ops:
  1.3 54.6 %shard_map.86 = (f32[192,192]{1,0:T(8,128)}, f32[1,1]{1,0:T(1,128)}) custom-call(bf16[30,192,192]{2,1,0:T(8,128)(2,1)} %bitcast.8, bf16[30,192,192]{2,1,0:T(8,128)(2,1)} %bitcast.9, bf16[192,192]{1,0:T(8,128)(2,1)} %bitcast.10, bf16[192,192]{1,0:T(8,128)(2,1)} %bitcast.11, f32[1,192]{1,0:T(1,128)} %bitcast.12, s32[1,30]{1,0:T(1,128)} %chg_in.1, ...), custom_call_target="tpu_custom_call" | custom-call | flops 3397386240 | bytes 4423680 | tf_op jit(solution)/shard_map/pallas_call | solution.py:537
  55.8 1.6 %copy.12 = f32[1,1,192,192]{3,2,1,0:T(8,128)} copy(f32[1,1,192,192]{3,2,1,0:T(8,128)} %bitcast.7) | data formatting | bytes 294912

commit v3 on v2

--- a/solution.py
+++ b/solution.py
@@ -119,52 +119,15 @@
     pad = ch_loc.shape[0] - width
     ch_loc[width:, :] = jnp.full((pad, size), rows[0, 0], jnp.int32).astype(f32)
 
-    pl.semaphore_wait(
-        barrier, grps - 1 + grps * (has_up.astype(jnp.int32) + has_dn.astype(jnp.int32)))
-
-    def site_up():
-        return remote(site_send.at[0], site_recv.at[0], site_s.at[0], site_r.at[0], seg=up)
-
-    def site_dn():
-        return remote(site_send.at[1], site_recv.at[1], site_s.at[1], site_r.at[1], seg=dn)
-
-    def ch_dn():
-        return remote(ch_loc, ch_rem, site_s.at[2], site_r.at[2], seg=dn)
-
-    def env_up(k):
-        return remote(send_a.at[k], recv_a.at[k], env_s.at[0, k], env_r.at[0, k], seg=up)
-
-    def env_dn(k):
-        return remote(send_b.at[k], recv_b.at[k], env_s.at[1, k], env_r.at[1, k], seg=dn)
-
-    @pl.when(has_up)
-    def _():
-        site_up().start()
-
-    @pl.when(has_dn)
-    def _():
-        site_dn().start()
-        ch_dn().start()
-
-    def send_chunk(k, carry):
+    def pack_chunk(k, carry):
         load_a(k).wait()
         load_b(k).wait()
-
-        @pl.when(has_up)
-        def _():
-            for j in range(chunk):
-                pack(send_a.at[k, j], elv[k * chunk + j])
-            env_up(k).start()
-
-        @pl.when(has_dn)
-        def _():
-            for j in range(chunk):
-                pack(send_b.at[k, j], erv[half + k * chunk + j])
-            env_dn(k).start()
-
+        for j in range(chunk):
+            pack(send_a.at[k, j], elv[k * chunk + j])
+            pack(send_b.at[k, j], erv[half + k * chunk + j])
         return carry
 
-    lax.fori_loop(0, chunks, send_chunk, 0)
+    lax.fori_loop(0, chunks, pack_chunk, 0)
     load_rest_a().wait()
     load_rest_b().wait()
 
@@ -176,6 +139,49 @@
     def _():
         for w in range(half):
             full_a[w] = (eye_block if w == 0 else jnp.zeros_like(eye_block)).astype(bf16)
+
+    for i in (upper, lower):
+        acc[i] = jnp.zeros(acc.shape[1:], f32)
+
+    pl.semaphore_wait(
+        barrier, grps - 1 + grps * (has_up.astype(jnp.int32) + has_dn.astype(jnp.int32)))
+
+    def site_up():
+        return remote(site_send.at[0], site_recv.at[0], site_s.at[0], site_r.at[0], seg=up)
+
+    def site_dn():
+        return remote(site_send.at[1], site_recv.at[1], site_s.at[1], site_r.at[1], seg=dn)
+
+    def ch_dn():
+        return remote(ch_loc, ch_rem, site_s.at[2], site_r.at[2], seg=dn)
+
+    def env_up(k):
+        return remote(send_a.at[k], recv_a.at[k], env_s.at[0, k], env_r.at[0, k], seg=up)
+
+    def env_dn(k):
+        return remote(send_b.at[k], recv_b.at[k], env_s.at[1, k], env_r.at[1, k], seg=dn)
+
+    @pl.when(has_up)
+    def _():
+        site_up().start()
+
+    @pl.when(has_dn)
+    def _():
+        site_dn().start()
+        ch_dn().start()
+
+    def send_chunk(k, carry):
+        @pl.when(has_up)
+        def _():
+            env_up(k).start()
+
+        @pl.when(has_dn)
+        def _():
+            env_dn(k).start()
+
+        return carry
+
+    lax.fori_loop(0, chunks, send_chunk, 0)
 
     row_f = row_at.astype(f32)
 
@@ -245,7 +251,6 @@
         basis = theta[i] / jnp.sqrt(norms[i : i + 1, :] + eps_value)
         theta[i] = basis
         v16[i] = basis.astype(bf16)
-        acc[i] = jnp.zeros(acc.shape[1:], f32)
 
     def one_term(a, v, ch_row, b):
         inner = jnp.dot(a, v, preferred_element_type=f32).astype(bf16)
@@ -385,14 +390,26 @@
         image[lower] = image[lower] + unpack(z_recv.at[lower], size).astype(f32)
 
     stat_start(1, [column_sums(theta[i] * image[i]) for i in (upper, lower)])
+    for i in (upper, lower):
+        v16[i] = image[i].astype(bf16)
+        acc[i] = jnp.zeros(acc.shape[1:], f32)
+
+    def upper_step(k, carry):
+        upper_chunk(k)
+        return carry
+
+    def lower_step(k, carry):
+        lower_chunk(k)
+        return carry
+
+    lax.fori_loop(0, chunks, upper_step, 0)
+
     diags = total(stat_finish(1))
     diag_one = diags[0:1, :]
 
     def send_res(role):
         residual = image[role] - diags[role : role + 1, :] * theta[role]
-        rounded = residual.astype(bf16)
-        v16[role] = rounded
-        pack(res_send.at[role], rounded)
+        pack(res_send.at[role], residual.astype(bf16))
 
         @pl.when(has_lo)
         def _():
@@ -408,21 +425,8 @@
 
     @pl.when(has_up)
     def _():
-        send_res(lower)
-
-    for i in (upper, lower):
-        acc[i] = jnp.zeros(acc.shape[1:], f32)
-
-    def second_chunk(k, carry):
-        upper_chunk(k)
-
-        @pl.when(has_up)
-        def _():
-            lower_chunk(k)
-
-        return carry
-
-    lax.fori_loop(0, chunks, second_chunk, 0)
+        image[lower] = send_res(lower)
+        lax.fori_loop(0, chunks, lower_step, 0)
 
     def overlap(role, own):
         theta_out[...] = own * slab(role, 1)
@@ -451,7 +455,7 @@
     @pl.when(has_up)
     def _():
         zero = jnp.zeros((1, size), f32)
-        low_send[...] = stat_tile([zero, zero, overlap(lower, v16[lower].astype(f32))])
+        low_send[...] = stat_tile([zero, zero, overlap(lower, image[lower])])
         for j in range(grps):
             low_copy(j).start()
 
@@ -476,7 +480,7 @@
     sums = total(stat_finish(2), low_recv)
     scale = 1.0 / jnp.sqrt(sums[0:1, :] + eps_value)
     coupling = sums[1:2, :] * scale
-    diag_two = sums[2:3, :] * scale * scale
+    diag_two = (sums[2:3, :] - diag_one * sums[1:2, :]) * scale * scale
     half_gap = 0.5 * (diag_one - diag_two)
     energy = 0.5 * (diag_one + diag_two) - jnp.sqrt(half_gap * half_gap + coupling * coupling)
     lead_coef = diag_two - energy

time: 59.4 us -> 58 us (0.976)
  Pallas kernels: 54.6 us -> 53.1 us
    pallas_call x1, Pallas kernels: 54.6 us -> 53.1 us  [body(): pl.pallas_call(functools.partial(kernel, segs, grps, chunk), out_shape=(j...]
where the time goes in v3:
time: 58 us; the launch traced here: 57.8 us
  Pallas kernels  53.1 us (92%)
  between operations  3.05 us (5%)
  local copies, waits for them, and re-layouts  1.62 us (3%)
    pallas_call x1, Pallas kernels, body(): pl.pallas_call(functools.partial(kernel, segs, grps, chunk), out_shape=(j...  53.1 us
    unnamed x1, local copies, waits for them, and re-layouts  1.62 us

profile of v3, /device:TPU:0, one launch (start us, length us, event | category | flops | bytes accessed | tf_op | source)
XLA Modules:
  0.0 57.8 jit_solution(5302287372251710429)
XLA Ops:
  1.3 53.1 %shard_map.86 = (f32[192,192]{1,0:T(8,128)}, f32[1,1]{1,0:T(1,128)}) custom-call(bf16[30,192,192]{2,1,0:T(8,128)(2,1)} %bitcast.8, bf16[30,192,192]{2,1,0:T(8,128)(2,1)} %bitcast.9, bf16[192,192]{1,0:T(8,128)(2,1)} %bitcast.10, bf16[192,192]{1,0:T(8,128)(2,1)} %bitcast.11, f32[1,192]{1,0:T(1,128)} %bitcast.12, s32[1,30]{1,0:T(1,128)} %chg_in.1, ...), custom_call_target="tpu_custom_call" | custom-call | flops 3397386240 | bytes 4423680 | tf_op jit(solution)/shard_map/pallas_call | solution.py:541
  54.4 1.6 %copy.12 = f32[1,1,192,192]{3,2,1,0:T(8,128)} copy(f32[1,1,192,192]{3,2,1,0:T(8,128)} %bitcast.7) | data formatting | bytes 294912

commit v4 on v3

--- a/solution.py
+++ b/solution.py
@@ -257,7 +257,7 @@
         parts = [inner * jnp.where(ch_row == c, 1.0, 0.0).astype(bf16) for c in (-1.0, 0.0, 1.0)]
         return jnp.dot(jnp.concatenate(parts, axis=0), b, preferred_element_type=f32)
 
-    def upper_chunk(k):
+    def upper_chunk(k, chunk=chunk):
         value = None
         for j in range(chunk):
             w = k * chunk + j
@@ -265,7 +265,7 @@
             value = term if value is None else value + term
         acc[upper] = acc[upper] + value
 
-    def lower_chunk(k):
+    def lower_chunk(k, chunk=chunk):
         value = None
         for j in range(chunk):
             w = k * chunk + j
@@ -394,15 +394,17 @@
         v16[i] = image[i].astype(bf16)
         acc[i] = jnp.zeros(acc.shape[1:], f32)
 
+    step = 5 if half % 5 == 0 else 1
+
     def upper_step(k, carry):
-        upper_chunk(k)
+        upper_chunk(k, step)
         return carry
 
     def lower_step(k, carry):
-        lower_chunk(k)
+        lower_chunk(k, step)
         return carry
 
-    lax.fori_loop(0, chunks, upper_step, 0)
+    lax.fori_loop(0, half // step, upper_step, 0)
 
     diags = total(stat_finish(1))
     diag_one = diags[0:1, :]
@@ -426,7 +428,7 @@
     @pl.when(has_up)
     def _():
         image[lower] = send_res(lower)
-        lax.fori_loop(0, chunks, lower_step, 0)
+        lax.fori_loop(0, half // step, lower_step, 0)
 
     def overlap(role, own):
         theta_out[...] = own * slab(role, 1)

time: 58 us -> 57.8 us (level)
  no operation moved by 1% of the time
where the time goes in v4:
time: 57.8 us; the launch traced here: 57.6 us
  Pallas kernels  52.9 us (92%)
  between operations  3.05 us (5%)
  local copies, waits for them, and re-layouts  1.62 us (3%)
    pallas_call x1, Pallas kernels, body(): pl.pallas_call(functools.partial(kernel, segs, grps, chunk), out_shape=(j...  52.9 us
    unnamed x1, local copies, waits for them, and re-layouts  1.62 us

profile of v4, /device:TPU:0, one launch (start us, length us, event | category | flops | bytes accessed | tf_op | source)
XLA Modules:
  0.0 57.6 jit_solution(2892270735260559756)
XLA Ops:
  1.3 52.9 %shard_map.86 = (f32[192,192]{1,0:T(8,128)}, f32[1,1]{1,0:T(1,128)}) custom-call(bf16[30,192,192]{2,1,0:T(8,128)(2,1)} %bitcast.8, bf16[30,192,192]{2,1,0:T(8,128)(2,1)} %bitcast.9, bf16[192,192]{1,0:T(8,128)(2,1)} %bitcast.10, bf16[192,192]{1,0:T(8,128)(2,1)} %bitcast.11, f32[1,192]{1,0:T(1,128)} %bitcast.12, s32[1,30]{1,0:T(1,128)} %chg_in.1, ...), custom_call_target="tpu_custom_call" | custom-call | flops 3397386240 | bytes 4423680 | tf_op jit(solution)/shard_map/pallas_call | solution.py:543
  54.2 1.6 %copy.12 = f32[1,1,192,192]{3,2,1,0:T(8,128)} copy(f32[1,1,192,192]{3,2,1,0:T(8,128)} %bitcast.7) | data formatting | bytes 294912
